TPU v7x, 256 devices: a whole 4x4x8 slice. The times are simulated.
256 devices in a mesh: rows: 64 (over x, z, core), cols: 4 (over y).
Axes of the slice: x: 4, y: 4, z: 8, core: 2. Of those that a mesh axis runs over, the one named last changes fastest.
Arguments:
- features: bfloat16 [2048, 32768], P('rows', 'cols'), may hold values from -6 to 6
- block_rows: int32 [2, 512, 8], P(None, 'cols'), may hold values from 0 to 511, as said below
- weights: bfloat16 [2, 256, 512, 128], P(None, 'cols', 'rows'), may hold values from -0.375 to 0.375
- biases: float32 [2, 32768], P(None, 'cols'), may hold values from -0.5 to 0.2
Outputs:
- activations: bfloat16 [2048, 32768], P('rows', 'cols')
Inputs may be any that keep to these rules, and one draw needn't show every extreme that they name: `block_rows`: the 8 block rows of one block column are distinct.
All inputs are finite; a program needn't handle non-finite values.
Results may differ from a plain program's by a relative error of at most 0.0051.
Values may be sent and summed in bfloat16 or wider, within the bound.
A program may use at most 128 MiB of HBM per device.

v0:
```python
import functools

import jax
import jax.numpy as jnp
from jax import lax
from jax.experimental import pallas as pl
from jax.experimental.pallas import tpu as pltpu
from jax.sharding import PartitionSpec as P

MESH = pl.DeviceIdType.MESH
NX, NY, NZ = 4, 4, 8
CHIPS = NX * NZ
PAIRS = 64
MINE = PAIRS // 2
HALF_ROWS = 32
ROWS = 2 * HALF_ROWS
LANES = 128
DIRS = ("x+", "x-", "z+", "z-")
SLOTS = 6

CHUNKS = (
    (0, 0, 3, 5, 1, 3),
    (0, 8, 3, 5, 2, 2),
    (0, 16, 4, 4, 2, 2),
    (0, 24, 3, 5, 1, 3),
    (1, 0, 3, 5, 2, 2),
    (1, 8, 4, 4, 2, 2),
    (1, 16, 3, 5, 1, 3),
    (1, 24, 3, 5, 2, 2),
)
PARTS = 4
ORDER = (
    ("own",), ("merge", 0), ("flood", 0, 1), ("flood", 2, 1), ("flood", 1, 1), ("merge", 1), ("flood", 4, 1),
    ("flood", 3, 1), ("flood", 0, 2), ("flood", 2, 2), ("flood", 1, 2), ("x", "+0"), ("flood", 3, 2), ("x", "-1"),
    ("flood", 0, 3), ("flood", 2, 3), ("flood", 5, 1), ("flood", 1, 3), ("flood", 0, 4), ("flood", 3, 3),
    ("flood", 2, 4), ("flood", 1, 4), ("x", "-0"), ("x", "+1"), ("x", "--1"), ("flood", 0, 5), ("x", "++0"),
    ("flood", 7, 1), ("flood", 3, 4), ("flood", 6, 1), ("x_all",), ("flood", 1, 5), ("flood", 0, 6), ("roll", 0),
    ("flood", 5, 2), ("roll", 2), ("flood", 2, 5), ("roll", 1), ("flood", 4, 2), ("roll", 3), ("flood", 1, 6),
    ("flood", 3, 5), ("flood", 0, 7), ("one", 0), ("flood", 6, 2), ("flood", 2, 6), ("flood", 7, 2), ("flood", 1, 7),
    ("one", 1), ("flood", 3, 6), ("flood", 4, 3), ("flood", 2, 7), ("flood", 6, 3), ("one", 2), ("flood", 5, 3),
    ("flood", 3, 7), ("y", "+", 0), ("flood", 7, 3), ("one", 3), ("flood", 6, 4), ("y", "-", 1), ("flood", 4, 4),
    ("y", "+", 1), ("flood", 5, 4), ("y_in", 0), ("y", "-", 2), ("flood", 7, 4), ("y", "-", 3), ("flood", 6, 5),
    ("flood", 4, 5), ("y", "-", 0), ("y", "+", 2), ("flood", 5, 5), ("flood", 7, 5), ("y", "+", 3), ("y", "++", 0),
    ("y", "--", 2), ("flood", 6, 6), ("flood", 4, 6), ("flood", 5, 6), ("y_in", 2), ("y", "++", 1), ("y", "--", 3),
    ("y_in", 1), ("flood", 7, 6), ("flood", 6, 7), ("y_in", 3), ("flood", 4, 7), ("two", 0), ("flood", 5, 7),
    ("two", 1), ("two", 2), ("flood", 7, 7), ("two", 3),
)


def pieces_of(chunk, slot, direction):
    _, first, n_a, n_b, a_cut, b_cut = chunk
    plus = direction[1] == "+"
    sign = 1 if plus else -1
    a_all, b_all = (first, n_a), (first + n_a, n_b)
    a_part = (first, a_cut) if plus else (first + a_cut, n_a - a_cut)
    b_part = (first + n_a, b_cut) if plus else (first + n_a + b_cut, n_b - b_cut)
    found = []
    if direction[0] == "z":
        columns = ((1, 0, a_all, a_part), (2, 1, a_all, a_part), (2, -1, a_all, a_part), (3, 2, a_all, a_part), (1, 0, b_all, b_part))
        for start, offset, whole, part in columns:
            step = slot - start
            if 0 <= step <= 2:
                found.append((offset, -sign * step, *whole))
            elif step == 3:
                found.append((offset, -sign * step, *part))
    else:
        if slot == 1:
            found.append((0, 0, *a_all))
        elif slot == 2:
            found.append((-sign, 0, *a_part))
        around = {0: (0,), 1: (1, -1), 2: (2, -2), 3: (3, -3), 4: (4,)}
        for far in around.get(slot - 1, ()):
            found.append((0, far, *b_all))
        for far in around.get(slot - 2, ()):
            found.append((-sign, far, *b_part))
    merged = []
    for piece in found:
        if piece[3] == 0:
            continue
        for at, other in enumerate(merged):
            if other[:2] == piece[:2] and other[2] + other[3] == piece[2]:
                merged[at] = (*other[:3], other[3] + piece[3])
                break
        else:
            merged.append(piece)
    return merged


def tiles_of(chunk, slot, direction):
    return sum(piece[3] for piece in pieces_of(chunk, slot, direction))


def kernel(
    index_ref, feat_ref, w_ref, bias_ref, out_ref,
    x_buf, y_buf, g_buf, w_buf, part_buf, away,
    flood_send, flood_recv, part_send, part_recv, x_send, x_recv, y_send, y_recv, out_send, out_recv, x_in, w_in,
):
    row, y = lax.axis_index("rows"), lax.axis_index("cols")
    core = row % 2
    z = (row // 2) % NZ
    x = row // (2 * NZ)

    def device(direction):
        nx, ny, nz, nc = x, y, z, core
        if direction == "c":
            nc = 1 - core
        else:
            step = 1 if direction[1] == "+" else -1
            if direction[0] == "x":
                nx = (x + step + NX) % NX
            elif direction[0] == "y":
                ny = (y + step + NY) % NY
            else:
                nz = (z + step + NZ) % NZ
        return ((nx * NZ + nz) * 2 + nc, ny)

    barrier = pltpu.get_barrier_semaphore()
    neighbours = DIRS + ("y+", "y-", "c")
    for direction in neighbours:
        pl.semaphore_signal(barrier, inc=1, device_id=device(direction), device_id_type=MESH)

    my_rows = pl.ds(pl.multiple_of(core * HALF_ROWS, HALF_ROWS), HALF_ROWS)
    w_copy = pltpu.make_async_copy(w_ref, w_buf, w_in)
    w_copy.start()

    def stage(step, carry):
        for more in range(8):
            pair = step * 8 + more
            columns = pl.ds(pl.multiple_of(pair * LANES, LANES), LANES)
            pltpu.make_async_copy(feat_ref.at[:, columns], x_buf.at[y * PAIRS + pair, 0, my_rows], x_in).start()
        return carry

    lax.fori_loop(0, PAIRS // 8, stage, 0)
    w_copy.wait()
    pl.semaphore_wait(barrier, len(neighbours))

    def part_copy(layer):
        theirs = pl.ds(pl.multiple_of((1 - core) * MINE * 8, MINE * 8), MINE * 8)
        return pltpu.make_async_remote_copy(
            w_buf.at[layer, theirs], part_buf.at[layer], part_send, part_recv.at[layer],
            device_id=device("c"), device_id_type=MESH,
        )

    part_copies = [part_copy(layer) for layer in range(2)]
    part_copies[0].start()

    def x_copy(number, offset, half, halves, direction):
        source = (y + offset + NY) % NY
        where = x_buf.at[pl.ds(source * PAIRS + half * (PAIRS // 2), halves * (PAIRS // 2)), 0, my_rows]
        return pltpu.make_async_remote_copy(
            where, where, x_send, x_recv.at[min(number, 6)], device_id=device(direction), device_id_type=MESH
        )

    x_copies = {
        "+0": x_copy(0, 0, 0, 1, "y+"),
        "-1": x_copy(1, 0, 1, 1, "y-"),
        "+1": x_copy(2, 0, 1, 1, "y+"),
        "-0": x_copy(3, 0, 0, 1, "y-"),
        "++0": x_copy(4, -1, 0, 1, "y+"),
        "--1": x_copy(5, 1, 1, 1, "y-"),
        "c": x_copy(6, 0, 0, 2, "c"),
        "c+0": x_copy(7, -1, 0, 1, "c"),
        "c-1": x_copy(8, 1, 1, 1, "c"),
        "c+1": x_copy(9, -1, 1, 1, "c"),
        "c-0": x_copy(10, 1, 0, 1, "c"),
        "c++0": x_copy(11, 2, 0, 1, "c"),
        "c--1": x_copy(12, 2, 1, 1, "c"),
    }
    part_copies[1].start()
    mine = x_buf.at[pl.ds(y * PAIRS, PAIRS), 0, my_rows]
    pltpu.make_async_copy(mine, mine, x_in).wait()

    def merge(layer):
        part_copies[layer].wait_recv()
        ours = pl.ds(pl.multiple_of(core * MINE * 8, MINE * 8), MINE * 8)
        own = w_buf[layer, ours, :].astype(jnp.float32).reshape(MINE, 8, LANES)
        other = part_buf[layer].astype(jnp.float32).reshape(MINE, 8, LANES)
        first = core == 0
        both = jnp.concatenate([jnp.where(first, own, other), jnp.where(first, other, own)], axis=1)
        base = ((layer * NX + x) * NZ + z) * MINE
        g_buf[pl.ds(base, MINE)] = both.astype(jnp.bfloat16)

    def flood_copy(number, slot, direction, piece):
        dx, dz, first, count = piece
        layer = CHUNKS[number][0]
        base = ((layer * NX + (x + dx + NX) % NX) * NZ + (z + dz + NZ) % NZ) * MINE + first
        where = g_buf.at[pl.ds(base, count)]
        return pltpu.make_async_remote_copy(
            where, where, flood_send, flood_recv.at[number, slot % 2], device_id=device(direction), device_id_type=MESH
        )

    def flood_issue(number, slot):
        for direction in DIRS:
            for piece in pieces_of(CHUNKS[number], slot, direction):
                flood_copy(number, slot, direction, piece).start()

    def counted(total, number, slot):
        where = g_buf.at[pl.ds(0, total)]
        return pltpu.make_async_remote_copy(
            where, where, flood_send, flood_recv.at[number, slot % 2], device_id=device("x+"), device_id_type=MESH
        )

    def flood_arrived(number, slot):
        counted(sum(tiles_of(CHUNKS[number], slot, direction) for direction in DIRS), number, slot).wait_recv()

    def flood_sent():
        counted(
            sum(
                tiles_of(chunk, slot, direction)
                for chunk in CHUNKS for slot in range(1, SLOTS + 1) for direction in DIRS
            ), 0, 1,
        ).wait_send()

    lane = lax.broadcasted_iota(jnp.int32, (ROWS, LANES), 1)
    low = lane < LANES // 2

    def change_over(panels, first, count):
        def step(at, carry):
            for more in range(8):
                pair = first + at * 8 + more
                panels[pair, 1] = pltpu.roll(panels[pair, 0], LANES // 2, 1)
            return carry

        lax.fori_loop(0, count // 8, step, 0)

    def pair_tile(layer, pair, panels):
        sides = []
        for h in range(2):
            column = (core * MINE + pair) * 2 + h
            tiles = []
            for k in range(0, 8, 2):
                one, two = index_ref[layer, k, column], index_ref[layer, k + 1, column]
                a, b = panels[one >> 1, one & 1], panels[two >> 1, 1 - (two & 1)]
                tiles.append(jnp.where(low, a, b))
            sides.append(jnp.concatenate(tiles, axis=1))
        picked = jnp.concatenate(sides, axis=0)
        w = jnp.concatenate([g_buf[(layer * CHIPS + chip) * MINE + pair] for chip in range(CHIPS)], axis=0)
        total = jnp.dot(picked, w, preferred_element_type=jnp.float32)
        total = jnp.where(low, total[:ROWS], total[ROWS:])
        total = total + bias_ref[layer : layer + 1, pl.ds(pl.multiple_of((core * MINE + pair) * LANES, LANES), LANES)]
        return jnp.maximum(total, 0.0).astype(jnp.bfloat16)

    share = MINE // PARTS

    def y_copy(number, offset, part, direction):
        source = (y + offset + NY) % NY
        where = y_buf.at[pl.ds(source * PAIRS + core * MINE + part * share, share), 0]
        return pltpu.make_async_remote_copy(
            where, where, y_send, y_recv.at[number], device_id=device(direction), device_id_type=MESH
        )

    y_copies = {}
    for part in range(PARTS):
        for number, way in enumerate(("c", "c+", "c-", "cc")):
            y_copies[way, part] = y_copy(number, (0, -1, 1, 2)[number], part, "c")
        y_copies["+", part] = y_copy(4 + part, 0, part, "y+")
        y_copies["-", part] = y_copy(4 + PARTS + part, 0, part, "y-")
        if part < PARTS // 2:
            y_copies["++", part] = y_copy(4 + 2 * PARTS + part, -1, part, "y+")
        else:
            y_copies["--", part] = y_copy(4 + 2 * PARTS + part, 1, part, "y-")

    def y_from_core(number):
        offset = (0, -1, 1, 2)[number]
        where = y_buf.at[pl.ds(0, MINE), 0]
        pltpu.make_async_remote_copy(
            where, where, y_send, y_recv.at[number], device_id=device("c"), device_id_type=MESH
        ).wait_recv()
        change_over(y_buf, (y + offset + NY) % NY * PAIRS + (1 - core) * MINE, MINE)

    def layer_one(part):
        def step(at, carry):
            pair = part * share + at
            tile = pair_tile(0, pair, x_buf)
            y_buf[y * PAIRS + core * MINE + pair, 0] = tile
            y_buf[y * PAIRS + core * MINE + pair, 1] = pltpu.roll(tile, LANES // 2, 1)
            return carry

        lax.fori_loop(0, share, step, 0, unroll=share)

    def layer_two(part):
        def step(at, carry):
            pair = part * share + at
            tile = pair_tile(1, pair, y_buf)
            first = core == 0
            ours = jnp.where(first, tile[:HALF_ROWS], tile[HALF_ROWS:])
            theirs = jnp.where(first, tile[HALF_ROWS:], tile[:HALF_ROWS])
            out_ref[:, pl.ds(pl.multiple_of((core * MINE + pair) * LANES, LANES), LANES)] = ours
            away[:, pl.ds(pl.multiple_of(pair * LANES, LANES), LANES)] = theirs
            return carry

        lax.fori_loop(0, share, step, 0, unroll=share)

    def out_copy(part):
        width = share * LANES
        there = pl.ds(pl.multiple_of((core * MINE + part * share) * LANES, width), width)
        return pltpu.make_async_remote_copy(
            away.at[:, pl.ds(part * width, width)], out_ref.at[:, there], out_send, out_recv,
            device_id=device("c"), device_id_type=MESH,
        )

    out_copies = [out_copy(part) for part in range(PARTS)]

    def x_step(name):
        x_copies[name].wait_recv()
        if name == "+0":
            x_copies["++0"].start()
        if name == "-1":
            x_copies["--1"].start()
        x_copies["c" + name].start()

    def y_step(way, part):
        y_copies[way, part].wait_recv()
        if (way, part < PARTS // 2) in (("+", True), ("-", False)):
            y_copies[way * 2, part].start()
        y_copies["cc" if len(way) == 2 else "c" + way, part].start()
        offset = {"+": -1, "-": 1}.get(way, 2)
        change_over(y_buf, (y + offset + NY) % NY * PAIRS + core * MINE + part * share, share)

    for task in ORDER:
        kind, *rest = task
        if kind == "own":
            for name in ("+0", "-1", "+1", "-0", "c"):
                x_copies[name].start()
        elif kind == "merge":
            merge(*rest)
        elif kind == "flood":
            number, slot = rest
            if slot > 1:
                flood_arrived(number, slot - 1)
            if slot <= SLOTS:
                flood_issue(number, slot)
        elif kind == "x":
            x_step(*rest)
        elif kind == "x_all":
            theirs = pl.ds(pl.multiple_of((1 - core) * HALF_ROWS, HALF_ROWS), HALF_ROWS)
            where = x_buf.at[:, 0, theirs]
            pltpu.make_async_remote_copy(
                where, where, x_send, x_recv.at[6], device_id=device("c"), device_id_type=MESH
            ).wait_recv()
        elif kind == "roll":
            (part,) = rest
            change_over(x_buf, part * PAIRS, PAIRS)
        elif kind == "one":
            (part,) = rest
            layer_one(part)
            for way in ("+", "-", "c"):
                y_copies[way, part].start()
        elif kind == "y":
            y_step(*rest)
        elif kind == "y_in":
            y_from_core(*rest)
        else:
            (part,) = rest
            layer_two(part)
            out_copies[part].start()

    whole = part_buf.at[:]
    pltpu.make_async_remote_copy(
        whole, whole, part_send, part_recv.at[0], device_id=device("c"), device_id_type=MESH
    ).wait_send()
    for buf, send, recv in ((x_buf, x_send, x_recv), (y_buf, y_send, y_recv)):
        moved = buf.at[pl.ds(0, 7 * MINE), 0]
        pltpu.make_async_remote_copy(
            moved, moved, send, recv.at[0], device_id=device("c"), device_id_type=MESH
        ).wait_send()
    flood_sent()
    pltpu.make_async_remote_copy(
        away, away, out_send, out_recv, device_id=device("c"), device_id_type=MESH
    ).wait()


def shards(features, block_rows, weights, biases):
    vmem = pl.BlockSpec(memory_space=pltpu.VMEM)
    anywhere = pl.BlockSpec(memory_space=pl.ANY)
    return pl.pallas_call(
        kernel,
        out_shape=jax.ShapeDtypeStruct((HALF_ROWS, PAIRS * LANES), jnp.bfloat16),
        in_specs=[pl.BlockSpec(memory_space=pltpu.SMEM), anywhere, anywhere, vmem],
        out_specs=vmem,
        scratch_shapes=[
            pltpu.VMEM((NY * PAIRS, 2, ROWS, LANES), jnp.bfloat16),
            pltpu.VMEM((NY * PAIRS, 2, ROWS, LANES), jnp.bfloat16),
            pltpu.VMEM((2 * CHIPS * MINE, 16, LANES), jnp.bfloat16),
            pltpu.VMEM((2, PAIRS * 8, LANES), jnp.bfloat16),
            pltpu.VMEM((2, MINE * 8, LANES), jnp.bfloat16),
            pltpu.VMEM((HALF_ROWS, MINE * LANES), jnp.bfloat16),
            pltpu.SemaphoreType.DMA,
            pltpu.SemaphoreType.DMA((len(CHUNKS), 2)),
            pltpu.SemaphoreType.DMA,
            pltpu.SemaphoreType.DMA((2,)),
            pltpu.SemaphoreType.DMA,
            pltpu.SemaphoreType.DMA((7,)),
            pltpu.SemaphoreType.DMA,
            pltpu.SemaphoreType.DMA((4 + 3 * PARTS,)),
            pltpu.SemaphoreType.DMA,
            pltpu.SemaphoreType.DMA,
            pltpu.SemaphoreType.DMA,
            pltpu.SemaphoreType.DMA,
        ],
        compiler_params=pltpu.CompilerParams(
            collective_id=0, has_side_effects=True, vmem_limit_bytes=56 << 20
        ),
    )(
        block_rows.transpose(0, 2, 1),
        features,
        weights.reshape(2, PAIRS * 8, LANES),
        biases,
    )


def solution(mesh):
    return jax.shard_map(
        shards,
        mesh=mesh,
        in_specs=(
            P("rows", "cols"),
            P(None, "cols", None),
            P(None, "cols", "rows", None),
            P(None, "cols"),
        ),
        out_specs=P("rows", "cols"),
        check_vma=False,
    )
```

profile of v0, /device:TPU:1, one launch (start us, length us, event | category | flops | bytes accessed | tf_op | source)
XLA Modules:
  0.0 68.4 jit_solution(11707289347794322652)
XLA Ops:
  0.0 66.5 %shard_map.46 = bf16[32,8192]{1,0:T(8,128)(2,1)} custom-call(s32[2,8,128]{2,1,0:T(8,128)} %bitcast.3, bf16[32,8192]{1,0:T(8,128)(2,1)} %feat_ref.1, bf16[2,512,128]{2,1,0:T(8,128)(2,1)} %bitcast.2, f32[2,8192]{1,0:T(2,128)} %bias_ref.1), custom_call_target="tpu_custom_call" | custom-call | tf_op jit(solution)/shard_map/pallas_call | solution.py:376
  66.5 1.9 %copy.6 = bf16[32,8192]{1,0:T(8,128)(2,1)} copy(bf16[32,8192]{1,0:T(8,128)(2,1)} %shard_map.46) | data formatting | bytes 1048576
where the time goes:
time: 68.6 us; the launch traced here: 68.4 us
  Pallas kernels  66.5 us (97%)
  local copies, waits for them, and re-layouts  1.87 us (3%)
    pallas_call x1, Pallas kernels, shards(): pl.pallas_call(kernel, out_shape=jax.ShapeDtypeStruct((HALF_ROWS, PAIRS *...  66.5 us
    unnamed x1, local copies, waits for them, and re-layouts  1.87 us

commit v1 on v0

--- a/solution.py
+++ b/solution.py
@@ -19,31 +19,35 @@
 SLOTS = 6
 
 CHUNKS = (
-    (0, 0, 3, 5, 1, 3),
+    (0, 0, 2, 2, 1, 1),
+    (0, 4, 1, 3, 0, 2),
     (0, 8, 3, 5, 2, 2),
     (0, 16, 4, 4, 2, 2),
     (0, 24, 3, 5, 1, 3),
     (1, 0, 3, 5, 2, 2),
     (1, 8, 4, 4, 2, 2),
     (1, 16, 3, 5, 1, 3),
-    (1, 24, 3, 5, 2, 2),
+    (1, 24, 1, 3, 1, 1),
+    (1, 28, 2, 2, 1, 1),
 )
 PARTS = 4
 ORDER = (
-    ("own",), ("merge", 0), ("flood", 0, 1), ("flood", 2, 1), ("flood", 1, 1), ("merge", 1), ("flood", 4, 1),
-    ("flood", 3, 1), ("flood", 0, 2), ("flood", 2, 2), ("flood", 1, 2), ("x", "+0"), ("flood", 3, 2), ("x", "-1"),
-    ("flood", 0, 3), ("flood", 2, 3), ("flood", 5, 1), ("flood", 1, 3), ("flood", 0, 4), ("flood", 3, 3),
-    ("flood", 2, 4), ("flood", 1, 4), ("x", "-0"), ("x", "+1"), ("x", "--1"), ("flood", 0, 5), ("x", "++0"),
-    ("flood", 7, 1), ("flood", 3, 4), ("flood", 6, 1), ("x_all",), ("flood", 1, 5), ("flood", 0, 6), ("roll", 0),
-    ("flood", 5, 2), ("roll", 2), ("flood", 2, 5), ("roll", 1), ("flood", 4, 2), ("roll", 3), ("flood", 1, 6),
-    ("flood", 3, 5), ("flood", 0, 7), ("one", 0), ("flood", 6, 2), ("flood", 2, 6), ("flood", 7, 2), ("flood", 1, 7),
-    ("one", 1), ("flood", 3, 6), ("flood", 4, 3), ("flood", 2, 7), ("flood", 6, 3), ("one", 2), ("flood", 5, 3),
-    ("flood", 3, 7), ("y", "+", 0), ("flood", 7, 3), ("one", 3), ("flood", 6, 4), ("y", "-", 1), ("flood", 4, 4),
-    ("y", "+", 1), ("flood", 5, 4), ("y_in", 0), ("y", "-", 2), ("flood", 7, 4), ("y", "-", 3), ("flood", 6, 5),
-    ("flood", 4, 5), ("y", "-", 0), ("y", "+", 2), ("flood", 5, 5), ("flood", 7, 5), ("y", "+", 3), ("y", "++", 0),
-    ("y", "--", 2), ("flood", 6, 6), ("flood", 4, 6), ("flood", 5, 6), ("y_in", 2), ("y", "++", 1), ("y", "--", 3),
-    ("y_in", 1), ("flood", 7, 6), ("flood", 6, 7), ("y_in", 3), ("flood", 4, 7), ("two", 0), ("flood", 5, 7),
-    ("two", 1), ("two", 2), ("flood", 7, 7), ("two", 3),
+    ("own",), ("merge", 0), ("flood", 0, 1), ("flood", 1, 1), ("flood", 2, 1), ("flood", 4, 1), ("merge", 1),
+    ("flood", 3, 1), ("flood", 8, 1), ("flood", 0, 2), ("flood", 1, 2), ("flood", 2, 2), ("flood", 3, 2),
+    ("flood", 0, 3), ("flood", 1, 3), ("x", "+0"), ("x", "-1"), ("flood", 2, 3), ("flood", 4, 2), ("flood", 3, 3),
+    ("flood", 1, 4), ("flood", 2, 4), ("x", "-0"), ("flood", 0, 4), ("flood", 5, 1), ("flood", 4, 3), ("flood", 8, 2),
+    ("flood", 2, 5), ("flood", 1, 5), ("x", "++0"), ("flood", 0, 5), ("x", "+1"), ("x", "--1"), ("flood", 3, 4),
+    ("flood", 4, 4), ("flood", 2, 6), ("flood", 9, 1), ("flood", 1, 6), ("x_all",), ("roll", 2), ("flood", 0, 6),
+    ("roll", 3), ("flood", 6, 1), ("flood", 7, 1), ("flood", 3, 5), ("flood", 5, 2), ("flood", 4, 5), ("roll", 0),
+    ("roll", 1), ("flood", 0, 7), ("flood", 2, 7), ("flood", 1, 7), ("one", 0), ("flood", 6, 2), ("flood", 3, 6),
+    ("flood", 7, 2), ("one", 1), ("flood", 5, 3), ("flood", 4, 6), ("flood", 9, 2), ("flood", 6, 3), ("flood", 3, 7),
+    ("one", 2), ("flood", 7, 3), ("flood", 8, 3), ("flood", 4, 7), ("one", 3), ("y", "-", 1), ("flood", 9, 3),
+    ("y", "+", 1), ("flood", 5, 4), ("flood", 6, 4), ("y", "-", 2), ("flood", 7, 4), ("y_in", 0), ("y", "+", 0),
+    ("flood", 9, 4), ("flood", 8, 4), ("y", "-", 3), ("flood", 5, 5), ("flood", 6, 5), ("flood", 7, 5),
+    ("flood", 9, 5), ("y", "--", 2), ("flood", 8, 5), ("y", "+", 3), ("y", "+", 2), ("y", "++", 1), ("flood", 5, 6),
+    ("flood", 6, 6), ("y", "-", 0), ("y", "--", 3), ("y", "++", 0), ("flood", 7, 6), ("flood", 9, 6), ("y_in", 2),
+    ("flood", 8, 6), ("y_in", 1), ("y_in", 3), ("flood", 5, 7), ("two", 0), ("flood", 6, 7), ("two", 1),
+    ("flood", 7, 7), ("two", 2), ("flood", 9, 7), ("flood", 8, 7), ("two", 3),
 )
 
 

time: 68.6 us -> 68.1 us (level)
  no operation moved by 1% of the time
where the time goes in v1:
time: 68.1 us; the launch traced here: 67.9 us
  Pallas kernels  66 us (97%)
  local copies, waits for them, and re-layouts  1.87 us (3%)
    pallas_call x1, Pallas kernels, shards(): pl.pallas_call(kernel, out_shape=jax.ShapeDtypeStruct((HALF_ROWS, PAIRS *...  66 us
    unnamed x1, local copies, waits for them, and re-layouts  1.87 us

profile of v1, /device:TPU:1, one launch (start us, length us, event | category | flops | bytes accessed | tf_op | source)
XLA Modules:
  0.0 67.9 jit_solution(7715348808834880370)
XLA Ops:
  0.0 66.0 %shard_map.46 = bf16[32,8192]{1,0:T(8,128)(2,1)} custom-call(s32[2,8,128]{2,1,0:T(8,128)} %bitcast.3, bf16[32,8192]{1,0:T(8,128)(2,1)} %feat_ref.1, bf16[2,512,128]{2,1,0:T(8,128)(2,1)} %bitcast.2, f32[2,8192]{1,0:T(2,128)} %bias_ref.1), custom_call_target="tpu_custom_call" | custom-call | tf_op jit(solution)/shard_map/pallas_call | solution.py:380
  66.0 1.9 %copy.6 = bf16[32,8192]{1,0:T(8,128)(2,1)} copy(bf16[32,8192]{1,0:T(8,128)(2,1)} %shard_map.46) | data formatting | bytes 1048576

commit v2 on v1

--- a/solution.py
+++ b/solution.py
@@ -32,7 +32,7 @@
 )
 PARTS = 4
 ORDER = (
-    ("own",), ("merge", 0), ("flood", 0, 1), ("flood", 1, 1), ("flood", 2, 1), ("flood", 4, 1), ("merge", 1),
+    ("own",), ("weights", 0), ("flood", 0, 1), ("flood", 1, 1), ("flood", 2, 1), ("flood", 4, 1), ("weights", 1),
     ("flood", 3, 1), ("flood", 8, 1), ("flood", 0, 2), ("flood", 1, 2), ("flood", 2, 2), ("flood", 3, 2),
     ("flood", 0, 3), ("flood", 1, 3), ("x", "+0"), ("x", "-1"), ("flood", 2, 3), ("flood", 4, 2), ("flood", 3, 3),
     ("flood", 1, 4), ("flood", 2, 4), ("x", "-0"), ("flood", 0, 4), ("flood", 5, 1), ("flood", 4, 3), ("flood", 8, 2),
@@ -174,15 +174,16 @@
     mine = x_buf.at[pl.ds(y * PAIRS, PAIRS), 0, my_rows]
     pltpu.make_async_copy(mine, mine, x_in).wait()
 
-    def merge(layer):
-        part_copies[layer].wait_recv()
-        ours = pl.ds(pl.multiple_of(core * MINE * 8, MINE * 8), MINE * 8)
-        own = w_buf[layer, ours, :].astype(jnp.float32).reshape(MINE, 8, LANES)
-        other = part_buf[layer].astype(jnp.float32).reshape(MINE, 8, LANES)
+    def merge(number):
+        layer, start, n_a, n_b, *_ = CHUNKS[number]
+        count = n_a + n_b
+        ours = pl.ds(pl.multiple_of((core * MINE + start) * 8, 32), count * 8)
+        own = w_buf[layer, ours, :].astype(jnp.float32).reshape(count, 8, LANES)
+        other = part_buf[layer, start * 8 : (start + count) * 8, :].astype(jnp.float32).reshape(count, 8, LANES)
         first = core == 0
         both = jnp.concatenate([jnp.where(first, own, other), jnp.where(first, other, own)], axis=1)
-        base = ((layer * NX + x) * NZ + z) * MINE
-        g_buf[pl.ds(base, MINE)] = both.astype(jnp.bfloat16)
+        base = ((layer * NX + x) * NZ + z) * MINE + start
+        g_buf[pl.ds(base, count)] = both.astype(jnp.bfloat16)
 
     def flood_copy(number, slot, direction, piece):
         dx, dz, first, count = piece
@@ -326,12 +327,14 @@
         if kind == "own":
             for name in ("+0", "-1", "+1", "-0", "c"):
                 x_copies[name].start()
-        elif kind == "merge":
-            merge(*rest)
+        elif kind == "weights":
+            part_copies[rest[0]].wait_recv()
         elif kind == "flood":
             number, slot = rest
             if slot > 1:
                 flood_arrived(number, slot - 1)
+            else:
+                merge(number)
             if slot <= SLOTS:
                 flood_issue(number, slot)
         elif kind == "x":

time: 68.1 us -> 68.1 us (level)
  no operation moved by 1% of the time
where the time goes in v2:
time: 68.1 us; the launch traced here: 67.9 us
  Pallas kernels  66 us (97%)
  local copies, waits for them, and re-layouts  1.87 us (3%)
    pallas_call x1, Pallas kernels, shards(): pl.pallas_call(kernel, out_shape=jax.ShapeDtypeStruct((HALF_ROWS, PAIRS *...  66 us
    unnamed x1, local copies, waits for them, and re-layouts  1.87 us

profile of v2, /device:TPU:1, one launch (start us, length us, event | category | flops | bytes accessed | tf_op | source)
XLA Modules:
  0.0 67.9 jit_solution(7175620832357040888)
XLA Ops:
  0.0 66.0 %shard_map.46 = bf16[32,8192]{1,0:T(8,128)(2,1)} custom-call(s32[2,8,128]{2,1,0:T(8,128)} %bitcast.3, bf16[32,8192]{1,0:T(8,128)(2,1)} %feat_ref.1, bf16[2,512,128]{2,1,0:T(8,128)(2,1)} %bitcast.2, f32[2,8192]{1,0:T(2,128)} %bias_ref.1), custom_call_target="tpu_custom_call" | custom-call | tf_op jit(solution)/shard_map/pallas_call | solution.py:383
  66.0 1.9 %copy.6 = bf16[32,8192]{1,0:T(8,128)(2,1)} copy(bf16[32,8192]{1,0:T(8,128)(2,1)} %shard_map.46) | data formatting | bytes 1048576

commit v3 on v1

--- a/solution.py
+++ b/solution.py
@@ -32,7 +32,7 @@
 )
 PARTS = 4
 ORDER = (
-    ("own",), ("merge", 0), ("flood", 0, 1), ("flood", 1, 1), ("flood", 2, 1), ("flood", 4, 1), ("merge", 1),
+    ("merge", 0), ("flood", 0, 1), ("own",), ("flood", 1, 1), ("flood", 2, 1), ("flood", 4, 1), ("merge", 1),
     ("flood", 3, 1), ("flood", 8, 1), ("flood", 0, 2), ("flood", 1, 2), ("flood", 2, 2), ("flood", 3, 2),
     ("flood", 0, 3), ("flood", 1, 3), ("x", "+0"), ("x", "-1"), ("flood", 2, 3), ("flood", 4, 2), ("flood", 3, 3),
     ("flood", 1, 4), ("flood", 2, 4), ("x", "-0"), ("flood", 0, 4), ("flood", 5, 1), ("flood", 4, 3), ("flood", 8, 2),
@@ -171,8 +171,6 @@
         "c--1": x_copy(12, 2, 1, 1, "c"),
     }
     part_copies[1].start()
-    mine = x_buf.at[pl.ds(y * PAIRS, PAIRS), 0, my_rows]
-    pltpu.make_async_copy(mine, mine, x_in).wait()
 
     def merge(layer):
         part_copies[layer].wait_recv()
@@ -324,6 +322,8 @@
     for task in ORDER:
         kind, *rest = task
         if kind == "own":
+            mine = x_buf.at[pl.ds(y * PAIRS, PAIRS), 0, my_rows]
+            pltpu.make_async_copy(mine, mine, x_in).wait()
             for name in ("+0", "-1", "+1", "-0", "c"):
                 x_copies[name].start()
         elif kind == "merge":

time: 68.1 us -> 68.3 us (level)
  no operation moved by 1% of the time
where the time goes in v3:
time: 68.3 us; the launch traced here: 68.1 us
  Pallas kernels  66.3 us (97%)
  local copies, waits for them, and re-layouts  1.87 us (3%)
    pallas_call x1, Pallas kernels, shards(): pl.pallas_call(kernel, out_shape=jax.ShapeDtypeStruct((HALF_ROWS, PAIRS *...  66.3 us
    unnamed x1, local copies, waits for them, and re-layouts  1.87 us

profile of v3, /device:TPU:1, one launch (start us, length us, event | category | flops | bytes accessed | tf_op | source)
XLA Modules:
  0.0 68.1 jit_solution(4846546616383122789)
XLA Ops:
  0.0 66.3 %shard_map.46 = bf16[32,8192]{1,0:T(8,128)(2,1)} custom-call(s32[2,8,128]{2,1,0:T(8,128)} %bitcast.3, bf16[32,8192]{1,0:T(8,128)(2,1)} %feat_ref.1, bf16[2,512,128]{2,1,0:T(8,128)(2,1)} %bitcast.2, f32[2,8192]{1,0:T(2,128)} %bias_ref.1), custom_call_target="tpu_custom_call" | custom-call | tf_op jit(solution)/shard_map/pallas_call | solution.py:380
  66.3 1.9 %copy.6 = bf16[32,8192]{1,0:T(8,128)(2,1)} copy(bf16[32,8192]{1,0:T(8,128)(2,1)} %shard_map.46) | data formatting | bytes 1048576
